TPU v7x, 32 devices: a whole 2x2x4 slice. The times are simulated.
32 devices in a mesh: axial: 8 (over z, core), circ: 4 (over y, x).
Axes of the slice: x: 2, y: 2, z: 4, core: 2. Of those that a mesh axis runs over, the one named last changes fastest.
Arguments:
- right_side: float32 [64, 64, 256], P('axial', 'circ'), may hold values from -6 to 6
- stiffness: float32 [64, 64, 256], P('axial', 'circ'), may hold values from 0.03 to 0.3
- material: int32 [64, 64, 256], P('axial', 'circ'), may hold values from 0 to 15
- groups: int32 [64, 64, 256], P('axial', 'circ'), may hold values from 0 to 7, as said below
Outputs:
- solution: float32 [64, 64, 256], P('axial', 'circ')
- residual: float32 [64, 64, 256], P('axial', 'circ')
Inputs may be any that keep to these rules, and one draw needn't show every extreme that they name: `groups`: in every column of cells along the third dimension every group number from 0 to 7 occurs.
All inputs are finite; a program needn't handle non-finite values.
Results may differ from a plain program's by a relative error of at most 0.0003.
Values sent between devices are 32-bit elements; how exact they have to be, the bound alone decides.
A program may use at most 128 MiB of HBM per device.

v0:
```python
import functools
import math

import jax
import jax.numpy as jnp
from jax import lax
from jax.experimental import pallas as pl
from jax.experimental.pallas import tpu as pltpu
from jax.sharding import PartitionSpec as P

LABELS = 8
ITERS = 2
MASS_SHIFT = 0.02
PRECISE = lax.Precision.HIGHEST
MESH = pl.DeviceIdType.MESH
PAD = 8
LANES = 128
VMEM = pl.BlockSpec(memory_space=pltpu.VMEM)
HALF_STEPS = (
    (0, 0, 1),
    (0, 1, -1),
    (0, 1, 0),
    (0, 1, 1),
    (1, -1, -1),
    (1, -1, 0),
    (1, -1, 1),
    (1, 0, -1),
    (1, 0, 0),
    (1, 0, 1),
    (1, 1, -1),
    (1, 1, 0),
    (1, 1, 1),
)


SIDES = tuple((a, c) for a in (-1, 0, 1) for c in (-1, 0, 1) if (a, c) != (0, 0))
PANELS = ((0, 0), (0, 1), (1, -1), (1, 0), (1, 1))


def params(collective_id=None):
    if collective_id is None:
        return pltpu.CompilerParams(vmem_limit_bytes=56 * 1024 * 1024)
    return pltpu.CompilerParams(
        vmem_limit_bytes=56 * 1024 * 1024, collective_id=collective_id, has_side_effects=True
    )


def halo_kernel(count, *refs):
    fields = refs[:count]
    out, send_circ, send_axial, send_corner, recv_circ, recv_axial, recv_corner, send_sem, recv_sem = refs[count:]
    rows_axial, rows_circ, depth = fields[0].shape
    axials, circs = lax.axis_size("axial"), lax.axis_size("circ")
    axial, circ = lax.axis_index("axial"), lax.axis_index("circ")

    def inside(move):
        return jnp.logical_and(axial + move >= 0, axial + move < axials)

    def peer(side):
        return (axial + side[0], lax.rem(circ + side[1] + circs, circs))

    barrier = pltpu.get_barrier_semaphore()
    for side in SIDES:
        @pl.when(inside(side[0]))
        def _():
            pl.semaphore_signal(barrier, inc=1, device_id=peer(side), device_id_type=MESH)

    for f in range(count):
        value = fields[f][...].astype(jnp.float32)
        send_axial[0, f] = value[0]
        send_axial[1, f] = value[rows_axial - 1]
        for c in range(2):
            row = c * (rows_circ - 1)
            face = value[:, row, :]
            send_circ[c, f] = face
            for a in range(2):
                x = a * (rows_axial - 1)
                send_corner[2 * a + c, f] = face[x : x + 1]

    ends = jnp.where(axial == 0, 1, 0) + jnp.where(axial == axials - 1, 1, 0)
    pl.semaphore_wait(barrier, len(SIDES) - 3 * ends)

    def copy(side):
        a, c = (side[0] + 1) // 2, (side[1] + 1) // 2
        if side[0] == 0:
            source, target = send_circ.at[c], recv_circ.at[1 - c]
        elif side[1] == 0:
            source, target = send_axial.at[a], recv_axial.at[1 - a]
        else:
            source, target = send_corner.at[2 * a + c], recv_corner.at[3 - 2 * a - c]
        number = SIDES.index(side)
        return pltpu.make_async_remote_copy(
            src_ref=source,
            dst_ref=target,
            send_sem=send_sem.at[number],
            recv_sem=recv_sem.at[number],
            device_id=peer(side),
            device_id_type=MESH,
        )

    for side in SIDES:
        @pl.when(inside(side[0]))
        def _():
            copy(side).start()

    for f in range(count):
        for x in (0, rows_axial + 1):
            out[f, x] = jnp.zeros((rows_circ + 2 * PAD, depth), jnp.float32)
        blank = jnp.zeros((rows_axial, PAD, depth), jnp.float32)
        out[f, 1 : rows_axial + 1, 0:PAD, :] = blank
        out[f, 1 : rows_axial + 1, PAD + rows_circ :, :] = blank
        out[f, 1 : rows_axial + 1, PAD : PAD + rows_circ, :] = fields[f][...].astype(jnp.float32)

    edge = (PAD - 1, PAD + rows_circ)
    for side in SIDES:
        a, c = (1 - side[0]) // 2, (1 - side[1]) // 2
        x = a * (rows_axial + 1)

        @pl.when(inside(-side[0]))
        def _():
            copy(side).wait_recv()
            for f in range(count):
                if side[0] == 0:
                    for row in range(rows_axial):
                        out[f, row + 1, edge[c] : edge[c] + 1, :] = recv_circ[c, f, row : row + 1, :]
                elif side[1] == 0:
                    out[f, x, PAD : PAD + rows_circ, :] = recv_axial[a, f]
                else:
                    out[f, x, edge[c] : edge[c] + 1, :] = recv_corner[2 * a + c, f]

    for side in SIDES:
        @pl.when(inside(side[0]))
        def _():
            copy(side).wait_send()


def halo(fields, collective_id):
    count = len(fields)
    rows_axial, rows_circ, depth = fields[0].shape
    buffers = [
        pltpu.VMEM((2, count, rows_axial, depth), jnp.float32),
        pltpu.VMEM((2, count, rows_circ, depth), jnp.float32),
        pltpu.VMEM((4, count, 1, depth), jnp.float32),
    ]
    return pl.pallas_call(
        functools.partial(halo_kernel, count),
        out_shape=jax.ShapeDtypeStruct(
            (count, rows_axial + 2, rows_circ + 2 * PAD, depth), jnp.float32
        ),
        in_specs=[VMEM] * count,
        out_specs=VMEM,
        scratch_shapes=buffers
        + buffers
        + [pltpu.SemaphoreType.DMA((len(SIDES),)), pltpu.SemaphoreType.DMA((len(SIDES),))],
        compiler_params=params(collective_id),
        name="halo",
    )(*fields)


def gather_kernel(own, out, send_sem, recv_sem):
    axials, circs = lax.axis_size("axial"), lax.axis_size("circ")
    devices = axials * circs
    me = lax.axis_index("axial") * circs + lax.axis_index("circ")

    def place(number):
        return (number // circs, lax.rem(number, circs))

    barrier = pltpu.get_barrier_semaphore()

    def greet(step, carry):
        pl.semaphore_signal(
            barrier, inc=1, device_id=place(lax.rem(me + step, devices)), device_id_type=MESH
        )
        return carry

    lax.fori_loop(1, devices, greet, 0)
    pl.semaphore_wait(barrier, devices - 1)

    def copy(step, slot):
        return pltpu.make_async_remote_copy(
            src_ref=own,
            dst_ref=out.at[slot],
            send_sem=send_sem.at[step],
            recv_sem=recv_sem.at[step],
            device_id=place(lax.rem(me + step, devices)),
            device_id_type=MESH,
        )

    def send(step, carry):
        copy(step, me).start()
        return carry

    lax.fori_loop(1, devices, send, 0)
    out[me] = own[...]

    def finish(step, carry):
        copy(step, lax.rem(me - step + devices, devices)).wait_recv()
        copy(step, me).wait_send()
        return carry

    lax.fori_loop(1, devices, finish, 0)


def gather(own, collective_id):
    devices = lax.axis_size("axial") * lax.axis_size("circ")
    out = pl.pallas_call(
        gather_kernel,
        out_shape=jax.ShapeDtypeStruct((devices,) + own.shape, jnp.float32),
        in_specs=[VMEM],
        out_specs=VMEM,
        scratch_shapes=[
            pltpu.SemaphoreType.DMA((devices,)),
            pltpu.SemaphoreType.DMA((devices,)),
        ],
        compiler_params=params(collective_id),
        name="gather",
    )(own)
    return out.reshape(devices * LABELS, LANES)


def shifted(window, move):
    if move == 0:
        return window
    depth = window.shape[-1]
    lane = lax.broadcasted_iota(jnp.int32, window.shape, window.ndim - 1)
    rolled = pltpu.roll(window, (depth - move) % depth, window.ndim - 1)
    return jnp.where(lane == (depth - 1 if move > 0 else 0), 0.0, rolled)


def window_of(ref, x, rows_circ, offset):
    return ref[x + 1 + offset[0], PAD + offset[1] : PAD + offset[1] + rows_circ, :]


def opposite(offset):
    return (-offset[0], -offset[1], -offset[2])


def terms():
    listed = []
    for position, offset in enumerate(HALF_STEPS):
        listed.append((position, offset))
        listed.append((len(HALF_STEPS) + position, opposite(offset)))
    return sorted(listed, key=lambda term: term[1])


def in_sums(sums):
    lane = lax.broadcasted_iota(jnp.int32, (LABELS, LANES), 1)
    tile = jnp.zeros((LABELS, LANES), jnp.float32)
    for position, value in sums:
        tile = tile + jnp.where(lane == position, value, 0.0)
    return tile


def label_sums(groups_ref, field_of, rows_axial, rows_circ, depth):
    def plane(x, sums):
        labels = window_of(groups_ref, x, rows_circ, (0, 0))
        value = field_of(x)
        return tuple(
            total + jnp.where(labels == float(label), value, 0.0)
            for label, total in enumerate(sums)
        )

    blank = jnp.zeros((rows_circ, depth), jnp.float32)
    sums = lax.fori_loop(0, rows_axial, plane, (blank,) * LABELS)
    rows = [jnp.sum(total, axis=0, keepdims=True) for total in sums]
    return jnp.sum(jnp.concatenate(rows, axis=0), axis=1, keepdims=True)


def weights_kernel(ext, right, weights, panel, stiff, seen, total):
    rows_axial, rows_circ, depth = right.shape
    groups = ext.at[2]
    half = len(HALF_STEPS)

    def stiffness_plane(x, carry):
        scale = ext[0, x]
        material = ext[1, x]
        upper = material >= 8.0
        angle = material - jnp.where(upper, 8.0, 0.0)
        first = jnp.full_like(scale, 1.0)
        second = jnp.zeros_like(scale)
        for turn in range(1, 8):
            first = jnp.where(angle == float(turn), math.cos(math.pi * turn / 8.0), first)
            second = jnp.where(angle == float(turn), math.sin(math.pi * turn / 8.0), second)
        shrink = jnp.where(upper, 0.6, 1.0)
        first, second = first * shrink, second * shrink
        third = jnp.where(upper, 0.8, 0.0)
        flat = scale * jnp.where(upper, 0.35 * 0.15, 0.15)
        along = scale * jnp.where(upper, 0.35 * 2.0, 6.0)
        for position, offset in enumerate(HALF_STEPS):
            length = float(sum(part * part for part in offset))
            dot = None
            for part, line in zip(offset, (first, second, third)):
                if part != 0:
                    line = line if part > 0 else -line
                    dot = line if dot is None else dot + line
            stiff[position, x] = flat * (1.0 / length) + along * (dot * dot) * (1.0 / (length * length))
        return carry

    lax.fori_loop(0, rows_axial + 2, stiffness_plane, 0)

    def weight_plane(x, carry):
        diagonal = None
        for position, offset in enumerate(HALF_STEPS):
            field = stiff.at[position]
            centre = window_of(field, x, rows_circ, (0, 0))
            ahead = 0.5 * (centre + shifted(window_of(field, x, rows_circ, offset), offset[2]))
            back = opposite(offset)
            behind = 0.5 * (centre + shifted(window_of(field, x, rows_circ, back), back[2]))
            weights[position, x] = ahead
            weights[half + position, x] = behind
            pair = ahead + behind
            diagonal = pair if diagonal is None else diagonal + pair
        weights[2 * half, x] = MASS_SHIFT + diagonal
        return carry

    lax.fori_loop(0, rows_axial, weight_plane, 0)

    row = lax.broadcasted_iota(jnp.int32, (rows_circ, depth), 0)
    listed = terms()
    total[...] = jnp.zeros_like(total)

    def own_labels(x):
        labels = window_of(groups, x, rows_circ, (0, 0))
        return jnp.concatenate(
            [jnp.where(labels == float(label), 1.0, 0.0) for label in range(LABELS)], axis=0
        )

    def seen_labels(offset, x):
        labels = window_of(groups, x, rows_circ, offset)
        if offset[2] == 0:
            return labels
        lane = lax.broadcasted_iota(jnp.int32, labels.shape, 1)
        rolled = pltpu.roll(labels, (depth - offset[2]) % depth, 1)
        return jnp.where(lane == (depth - 1 if offset[2] > 0 else 0), -1.0, rolled)

    def add_panel(slot, x, parts):
        found = jnp.concatenate(parts, axis=0)
        total[slot] += lax.dot_general(
            own_labels(x),
            found,
            (((1,), (1,)), ((), ())),
            precision=PRECISE,
            preferred_element_type=jnp.float32,
        )

    def panel_plane(x, carry):
        for number, (position, offset) in enumerate(listed):
            labels = seen_labels(offset, x)
            leaves = None
            if offset[1] != 0:
                leaves = row == (rows_circ - 1 if offset[1] > 0 else 0)
            if offset[0] != 0:
                edge = x == (rows_axial - 1 if offset[0] > 0 else 0)
                labels = jnp.where(edge, -1.0, labels)
            seen[number] = labels if leaves is None else jnp.where(leaves, -1.0, labels)
        parts, beside = [], []
        centre = window_of(groups, x, rows_circ, (0, 0))
        for label in range(LABELS):
            found = jnp.where(centre == float(label), weights[2 * half, x], 0.0)
            for number, (position, offset) in enumerate(listed):
                found = found - jnp.where(seen[number] == float(label), weights[position, x], 0.0)
            parts.append(found)
        add_panel(0, x, parts)
        for number, (position, offset) in enumerate(listed):
            if offset[1] > 0:
                labels = seen_labels(offset, x)
                if offset[0] != 0:
                    edge = x == (rows_axial - 1 if offset[0] > 0 else 0)
                    labels = jnp.where(edge, -1.0, labels)
                seen[number] = jnp.where(row == rows_circ - 1, labels, -1.0)
        for label in range(LABELS):
            found = jnp.zeros((rows_circ, depth), jnp.float32)
            for number, (position, offset) in enumerate(listed):
                if offset[1] > 0:
                    found = found - jnp.where(
                        seen[number] == float(label), weights[position, x], 0.0
                    )
            beside.append(found)
        add_panel(1, x, beside)
        return carry

    lax.fori_loop(0, rows_axial, panel_plane, 0)

    last = rows_axial - 1
    for slot in range(2, len(PANELS)):
        move = PANELS[slot][1]
        chosen = []
        for position, offset in listed:
            if offset[0] > 0 and (offset[1] == move or move == 0):
                labels = seen_labels(offset, last)
                if offset[1] != 0:
                    leaves = row == (rows_circ - 1 if offset[1] > 0 else 0)
                    labels = jnp.where(leaves == (move != 0), labels, -1.0)
                chosen.append((position, labels))
        parts = []
        for label in range(LABELS):
            found = jnp.zeros((rows_circ, depth), jnp.float32)
            for position, labels in chosen:
                found = found - jnp.where(labels == float(label), weights[position, last], 0.0)
            parts.append(found)
        add_panel(slot, last, parts)

    size = LABELS * rows_circ
    line = lax.broadcasted_iota(jnp.int32, (size, size), 0)
    column = lax.broadcasted_iota(jnp.int32, (size, size), 1)
    same = lax.rem(line, rows_circ) == lax.rem(column, rows_circ)
    tile_row = lax.broadcasted_iota(jnp.int32, (LABELS, size), 0)
    tile_column = lax.broadcasted_iota(jnp.int32, (LABELS, size), 1)
    collect = jnp.where(tile_column // rows_circ == tile_row, 1.0, 0.0)
    spot_row = lax.broadcasted_iota(jnp.int32, (size, LANES), 0)
    spot_column = lax.broadcasted_iota(jnp.int32, (size, LANES), 1)
    result = jnp.zeros((LABELS, LANES), jnp.float32)
    for slot in range(len(PANELS)):
        lines = jnp.dot(collect, jnp.where(same, total[slot], 0.0), precision=PRECISE)
        spots = jnp.where(spot_row // rows_circ + slot * LABELS == spot_column, 1.0, 0.0)
        result = result + jnp.dot(lines, spots, precision=PRECISE)
    own = label_sums(groups, lambda x: right[x], rows_axial, rows_circ, depth)
    panel[...] = result + in_sums([(len(PANELS) * LABELS, own)])


def inverse_of(matrix):
    size = matrix.shape[0]
    line = lax.broadcasted_iota(jnp.int32, (size, size), 0)
    column = lax.broadcasted_iota(jnp.int32, (size, size), 1)
    for step in range(size):
        pivot = 1.0 / matrix[step : step + 1, step : step + 1]
        across = matrix[step : step + 1, :] * pivot
        down = matrix[:, step : step + 1]
        in_line, in_column = line == step, column == step
        rest = jnp.where(in_column, 0.0, matrix) - down * jnp.where(in_column[0:1], pivot, across)
        matrix = jnp.where(in_line, jnp.where(in_column, pivot, across), rest)
    return matrix


def coarse_kernel(cycles, gathered, inverse, diagonals, uppers, held, linked, partial):
    size = gathered.shape[0] // cycles
    whole = gathered.shape[0]
    circs = size // LABELS
    line = lax.broadcasted_iota(jnp.int32, (size, size), 0) // LABELS
    column = lax.broadcasted_iota(jnp.int32, (size, size), 1) // LABELS
    spread_row = lax.broadcasted_iota(jnp.int32, (LANES, size), 0)
    spread_column = lax.rem(lax.broadcasted_iota(jnp.int32, (LANES, size), 1), LABELS)

    def dot(left, right):
        return jnp.dot(left, right, precision=PRECISE, preferred_element_type=jnp.float32)

    def block(s, slot):
        tiles = jnp.where(spread_row == spread_column + slot * LABELS, 1.0, 0.0)
        placed = dot(gathered[pl.ds(s * size, size), :], tiles)
        return jnp.where(lax.rem(line + PANELS[slot][1] + circs, circs) == column, placed, 0.0)

    def assemble(s, carry):
        beside = block(s, 1)
        diagonals[s] = block(s, 0) + beside + beside.T
        uppers[s] = block(s, 2) + block(s, 3) + block(s, 4)
        return carry

    lax.fori_loop(0, cycles, assemble, 0)
    unit_line = lax.broadcasted_iota(jnp.int32, (size, whole), 0)
    unit_column = lax.broadcasted_iota(jnp.int32, (size, whole), 1)

    def unit(s):
        return jnp.where(unit_line + s * size == unit_column, 1.0, 0.0)

    def eliminate(s, s_next, upper):
        inverted = inverse_of(diagonals[s])
        link = dot(inverted, upper)
        held[s] = inverted
        linked[s] = link
        across = upper.T
        diagonals[s_next] = diagonals[s_next] - dot(across, link)
        partial[s_next] = partial[s_next] - dot(link.T, partial[s])

    def start(s, carry):
        partial[s] = unit(s)
        return carry

    lax.fori_loop(0, cycles, start, 0)
    middle = cycles // 2

    def from_both_ends(step, carry):
        low, high = step, cycles - 1 - step
        upper_low, upper_high = uppers[low], uppers[high - 1].T
        inverted_low, inverted_high = inverse_pair(diagonals[low], diagonals[high])
        for s, s_next, upper, inverted in (
            (low, low + 1, upper_low, inverted_low),
            (high, high - 1, upper_high, inverted_high),
        ):
            link = dot(inverted, upper)
            held[s] = inverted
            linked[s] = link
            diagonals[s_next] = diagonals[s_next] - dot(upper.T, link)
            partial[s_next] = partial[s_next] - dot(link.T, partial[s])
        return carry

    lax.fori_loop(0, middle - 1, from_both_ends, 0)
    eliminate(middle - 1, middle, uppers[middle - 1])
    rows = pl.ds(middle * size, size)
    inverse[rows, :] = dot(inverse_of(diagonals[middle]), partial[middle])

    def put(s, s_next):
        ahead = inverse[pl.ds(s_next * size, size), :]
        inverse[pl.ds(s * size, size), :] = dot(held[s], partial[s]) - dot(linked[s], ahead)

    put(middle - 1, middle)

    def back(step, carry):
        put(middle - 2 - step, middle - 1 - step)
        put(middle + 1 + step, middle + step)
        return carry

    lax.fori_loop(0, middle - 1, back, 0)


def inverse_pair(first, second):
    return inverse_of(first), inverse_of(second)


def coarse_inverse(gathered):
    cycles, circs = lax.axis_size("axial"), lax.axis_size("circ")
    size, whole = circs * LABELS, gathered.shape[0]
    square = pltpu.VMEM((cycles, size, size), jnp.float32)
    return pl.pallas_call(
        functools.partial(coarse_kernel, cycles),
        out_shape=jax.ShapeDtypeStruct((whole, whole), jnp.float32),
        in_specs=[VMEM],
        out_specs=VMEM,
        scratch_shapes=[square] * 4 + [pltpu.VMEM((cycles, size, whole), jnp.float32)],
        compiler_params=params(),
        name="coarse_inverse",
    )(gathered)


def apply_plane(ext, weights, x, rows_circ):
    centre = 2 * len(HALF_STEPS)
    result = weights[centre, x] * window_of(ext, x, rows_circ, (0, 0))
    for position, offset in terms():
        value = shifted(window_of(ext, x, rows_circ, offset), offset[2])
        result = result - weights[position, x] * value
    return result


def spread_into(spread, values, column, groups):
    planes, rows, depth = spread.shape
    axials, circs = lax.axis_size("axial"), lax.axis_size("circ")
    axial, circ = lax.axis_index("axial"), lax.axis_index("circ")
    row = lax.broadcasted_iota(jnp.int32, (rows, depth), 0)

    def tile(a, c):
        at = axial + a
        present = jnp.logical_and(at >= 0, at < axials)
        at = jnp.minimum(jnp.maximum(at, 0), axials - 1)
        number = at * circs + lax.rem(circ + c + circs, circs)
        part = values[pl.ds(pl.multiple_of(number * LABELS, LABELS), LABELS), column : column + 1]
        return jnp.where(present, jnp.broadcast_to(part, (LABELS, depth)), 0.0)

    def fill(x, sides):
        labels = groups[x]
        value = jnp.zeros((rows, depth), jnp.float32)
        for label in range(LABELS):
            before, here, after = [side[label : label + 1, :] for side in sides]
            chosen = jnp.where(row < PAD, before, jnp.where(row < rows - PAD, here, after))
            value = jnp.where(labels == float(label), chosen, value)
        spread[x] = value

    fill(0, [tile(-1, c) for c in (-1, 0, 1)])
    fill(planes - 1, [tile(1, c) for c in (-1, 0, 1)])
    sides = [tile(0, c) for c in (-1, 0, 1)]

    def inner(x, carry):
        fill(x, sides)
        return carry

    lax.fori_loop(1, planes - 1, inner, 0)


def start_kernel(inverse, gathered, ext, weights, right, solution, residual, values, spread):
    rows_axial, rows_circ, depth = right.shape
    values[...] = jnp.dot(inverse[...], gathered[...], precision=PRECISE)
    spread_into(spread, values, len(PANELS) * LABELS, ext.at[2])

    def plane(x, carry):
        solution[x] = window_of(spread, x, rows_circ, (0, 0))
        residual[x] = right[x] - apply_plane(spread, weights, x, rows_circ)
        return carry

    lax.fori_loop(0, rows_axial, plane, 0)


def image_kernel(later, *refs):
    if later:
        residual_ext, ext, weights, direction_image, image, sums = refs
    else:
        residual_ext, ext, weights, image, sums = refs
    rows_axial, rows_circ, depth = image.shape
    field = residual_ext.at[0]

    def plane(x, totals):
        value = apply_plane(field, weights, x, rows_circ)
        image[x] = value
        residual = window_of(field, x, rows_circ, (0, 0))
        factors = [residual, value] + ([direction_image[x]] if later else [])
        return tuple(total + residual * factor for total, factor in zip(totals, factors))

    blank = jnp.zeros((rows_circ, depth), jnp.float32)
    totals = lax.fori_loop(0, rows_axial, plane, (blank,) * (3 if later else 2))
    found = [(0, label_sums(ext.at[2], lambda x: image[x], rows_axial, rows_circ, depth))]
    line = lax.broadcasted_iota(jnp.int32, (LABELS, LANES), 0)
    for position, total in enumerate(totals):
        whole = jnp.sum(jnp.sum(total, axis=0, keepdims=True), axis=1, keepdims=True)
        found.append((position + 1, jnp.where(line == 0, whole, 0.0)))
    sums[...] = in_sums(found)


def update_kernel(later, final, *refs):
    inverse, gathered, ext, weights, solution, residual, image = refs[:7]
    refs = refs[7:]
    if later:
        direction, direction_image, scalars = refs[:3]
        refs = refs[3:]
    solution_out, residual_out = refs[:2]
    refs = refs[2:]
    if not final:
        direction_out, direction_image_out, scalars_out = refs[:3]
        refs = refs[3:]
    values, spread = refs
    rows_axial, rows_circ, depth = solution.shape
    values[...] = jnp.dot(inverse[...], gathered[...], precision=PRECISE)
    spread_into(spread, values, 0, ext.at[2])
    totals = jnp.sum(gathered[...], axis=0, keepdims=True)
    norm = totals[:, 1:2]
    overlap = jnp.sum(gathered[...] * values[...], axis=0, keepdims=True)[:, 0:1]
    curvature = totals[:, 2:3] - overlap
    if later:
        ratio = norm / scalars[0:1, 0:1]
        curvature = ratio * ratio * scalars[0:1, 1:2] + 2.0 * ratio * totals[:, 3:4] + curvature
    step = norm / curvature

    def plane(x, carry):
        now = residual[x]
        along = now - window_of(spread, x, rows_circ, (0, 0))
        along_image = image[x] - apply_plane(spread, weights, x, rows_circ)
        if later:
            along = along + ratio * direction[x]
            along_image = along_image + ratio * direction_image[x]
        solution_out[x] = solution[x] + step * along
        residual_out[x] = now - step * along_image
        if not final:
            direction_out[x] = along
            direction_image_out[x] = along_image
        return carry

    lax.fori_loop(0, rows_axial, plane, 0)
    if not final:
        scalars_out[...] = in_sums([(0, norm), (1, curvature)])


def call(kernel, outs, scratch, args, name):
    return pl.pallas_call(
        kernel,
        out_shape=[jax.ShapeDtypeStruct(shape, jnp.float32) for shape in outs],
        in_specs=[VMEM] * len(args),
        out_specs=[VMEM] * len(outs),
        scratch_shapes=[pltpu.VMEM(shape, jnp.float32) for shape in scratch],
        compiler_params=params(),
        name=name,
    )(*args)


def shards(right_side, stiffness, material, groups):
    block = right_side.shape
    rows_axial, rows_circ, depth = block
    padded = (rows_axial + 2, rows_circ + 2 * PAD, depth)
    count = 2 * len(HALF_STEPS) + 1
    tile = (LABELS, LANES)
    size = LABELS * rows_circ
    ext = halo([stiffness, material, groups], 0)
    weights, panel = call(
        weights_kernel,
        [(count,) + block, tile],
        [(len(HALF_STEPS),) + padded, (count, rows_circ, depth), (len(PANELS), size, size)],
        [ext, right_side],
        "weights",
    )
    gathered = gather(panel, 1)
    inverse = coarse_inverse(gathered)
    work = [gathered.shape, padded]
    solution, residual = call(
        start_kernel, [block, block], work, [inverse, gathered, ext, weights, right_side], "start"
    )
    carried = []
    for iteration in range(ITERS):
        later, final = iteration > 0, iteration + 1 == ITERS
        residual_ext = halo([residual], 2 + 2 * iteration)
        image, sums = call(
            functools.partial(image_kernel, later),
            [block, tile],
            [],
            [residual_ext, ext, weights] + carried[1:2],
            "image",
        )
        gathered = gather(sums, 3 + 2 * iteration)
        solution, residual, *carried = call(
            functools.partial(update_kernel, later, final),
            [block, block] + ([] if final else [block, block, tile]),
            work,
            [inverse, gathered, ext, weights, solution, residual, image] + carried,
            "update",
        )
    return (solution, residual)


def solution(mesh):
    in_specs = (
        P("axial", "circ", None),
        P("axial", "circ", None),
        P("axial", "circ", None),
        P("axial", "circ", None),
    )
    out_specs = (P("axial", "circ", None), P("axial", "circ", None))
    return jax.shard_map(shards, mesh=mesh, in_specs=in_specs, out_specs=out_specs, check_vma=False)
```

profile of v0, /device:TPU:0, one launch (start us, length us, event | category | flops | bytes accessed | tf_op | source)
XLA Modules:
  0.0 129.4 jit_solution(15028354840806124651)
XLA Ops:
  0.6 8.8 %halo.3.ext.refs_1_.refs_2_ = f32[3,10,32,256]{3,2,1,0:T(8,128)} custom-call(f32[8,16,256]{2,1,0:T(8,128)} %refs_0_.1, s32[8,16,256]{2,1,0:T(8,128)} %refs_1_.1, s32[8,16,256]{2,1,0:T(8,128)} %refs_2_.1), custom_call_target="tpu_custom_call" | custom-call | tf_op jit(solution)/shard_map/halo/pallas_call | solution.py:144
  9.4 13.5 %weights.1 = (f32[27,8,16,256]{3,2,1,0:T(8,128)}, f32[8,128]{1,0:T(8,128)}) custom-call(f32[3,10,32,256]{3,2,1,0:T(8,128)} %halo.3.ext.refs_1_.refs_2_, f32[8,16,256]{2,1,0:T(8,128)} %right.3), custom_call_target="tpu_custom_call" | custom-call | tf_op jit(solution)/shard_map/weights/pallas_call | solution.py:658
  23.0 10.5 %gather.3 = f32[32,8,128]{2,1,0:T(8,128)} custom-call(f32[8,128]{1,0:T(8,128)} %get-tuple-element.15.own), custom_call_target="tpu_custom_call" | custom-call | tf_op jit(solution)/shard_map/gather/pallas_call | solution.py:205
  33.4 36.9 %coarse_inverse.1.inverse.refs_0_ = f32[256,256]{1,0:T(8,128)} custom-call(f32[256,128]{1,0:T(8,128)} %bitcast.3), custom_call_target="tpu_custom_call" | custom-call | tf_op jit(solution)/shard_map/coarse_inverse/pallas_call | solution.py:522
  70.3 5.0 %start.1 = (f32[8,16,256]{2,1,0:T(8,128)}, f32[8,16,256]{2,1,0:T(8,128)}) custom-call(f32[256,256]{1,0:T(8,128)} %coarse_inverse.1.inverse.refs_0_, f32[256,128]{1,0:T(8,128)} %bitcast.4, f32[3,10,32,256]{3,2,1,0:T(8,128)} %halo.3.ext.refs_1_.refs_2_, f32[27,8,16,256]{3,2,1,0:T(8,128)} %get-tuple-element.16.weights.refs_2_.refs_3_, f32[8,16,256]{2,1,0:T(8,128)} %right.3), custom_call_target="tpu_custom_call" | custom-call | tf_op jit(solution)/shard_map/start/pallas_call | solution.py:658
  75.3 6.8 %halo.4.refs_0_ = f32[1,10,32,256]{3,2,1,0:T(8,128)} custom-call(f32[8,16,256]{2,1,0:T(8,128)} %get-tuple-element.17.refs_0_.refs_5_), custom_call_target="tpu_custom_call" | custom-call | tf_op jit(solution)/shard_map/halo/pallas_call | solution.py:144
  82.1 4.5 %image.2 = (f32[8,16,256]{2,1,0:T(8,128)}, f32[8,128]{1,0:T(8,128)}) custom-call(f32[1,10,32,256]{3,2,1,0:T(8,128)} %halo.4.refs_0_, f32[3,10,32,256]{3,2,1,0:T(8,128)} %halo.3.ext.refs_1_.refs_2_, f32[27,8,16,256]{3,2,1,0:T(8,128)} %get-tuple-element.16.weights.refs_2_.refs_3_), custom_call_target="tpu_custom_call" | custom-call | tf_op jit(solution)/shard_map/image/pallas_call | solution.py:658
  86.6 10.4 %gather.4 = f32[32,8,128]{2,1,0:T(8,128)} custom-call(f32[8,128]{1,0:T(8,128)} %get-tuple-element.18.own), custom_call_target="tpu_custom_call" | custom-call | tf_op jit(solution)/shard_map/gather/pallas_call | solution.py:205
  96.9 5.4 %update.2 = (f32[8,16,256]{2,1,0:T(8,128)}, f32[8,16,256]{2,1,0:T(8,128)}, f32[8,16,256]{2,1,0:T(8,128)}, f32[8,16,256]{2,1,0:T(8,128)}, f32[8,128]{1,0:T(8,128)}) custom-call(f32[256,256]{1,0:T(8,128)} %coarse_inverse.1.inverse.refs_0_, f32[256,128]{1,0:T(8,128)} %bitcast.6, f32[3,10,32,256]{3,2,1,0:T(8,128)} %halo.3.ext.refs_1_.refs_2_, ...), custom_call_target="tpu_custom_call" | custom-call | tf_op jit(solution)/shard_map/update/pallas_call | solution.py:658
  102.3 6.8 %halo.5.refs_0_ = f32[1,10,32,256]{3,2,1,0:T(8,128)} custom-call(f32[8,16,256]{2,1,0:T(8,128)} %get-tuple-element.21.refs_0_.refs_5_), custom_call_target="tpu_custom_call" | custom-call | tf_op jit(solution)/shard_map/halo/pallas_call | solution.py:144
  109.2 4.5 %image.3 = (f32[8,16,256]{2,1,0:T(8,128)}, f32[8,128]{1,0:T(8,128)}) custom-call(f32[1,10,32,256]{3,2,1,0:T(8,128)} %halo.5.refs_0_, f32[3,10,32,256]{3,2,1,0:T(8,128)} %halo.3.ext.refs_1_.refs_2_, f32[27,8,16,256]{3,2,1,0:T(8,128)} %get-tuple-element.16.weights.refs_2_.refs_3_, f32[8,16,256]{2,1,0:T(8,128)} %get-tuple-element.22.refs_3_.refs_8_), custom_call_target="tpu_custom_call" | custom-call | tf_op jit(solution)/shard_map/image/pallas_call | solution.py:658
  113.7 10.4 %gather.5 = f32[32,8,128]{2,1,0:T(8,128)} custom-call(f32[8,128]{1,0:T(8,128)} %get-tuple-element.23.own), custom_call_target="tpu_custom_call" | custom-call | tf_op jit(solution)/shard_map/gather/pallas_call | solution.py:205
  124.0 5.4 %update.3 = (f32[8,16,256]{2,1,0:T(8,128)}, f32[8,16,256]{2,1,0:T(8,128)}) custom-call(f32[256,256]{1,0:T(8,128)} %coarse_inverse.1.inverse.refs_0_, f32[256,128]{1,0:T(8,128)} %bitcast.5, f32[3,10,32,256]{3,2,1,0:T(8,128)} %halo.3.ext.refs_1_.refs_2_, f32[27,8,16,256]{3,2,1,0:T(8,128)} %get-tuple-element.16.weights.refs_2_.refs_3_, ...), custom_call_target="tpu_custom_call" | custom-call | tf_op jit(solution)/shard_map/update/pallas_call | solution.py:658
where the time goes:
time: 130 us; the launch traced here: 129 us
  Pallas kernels  129 us (99%)
    pallas_call x6, Pallas kernels, call(): pl.pallas_call(kernel, out_shape=[jax.ShapeDtypeStruct(shape, jnp.float32...  38.3 us
    pallas_call x1, Pallas kernels, coarse_inverse(): pl.pallas_call(functools.partial(coarse_kernel, cycles), out_shape=jax.Sh...  36.9 us
    pallas_call x3, Pallas kernels, gather(): pl.pallas_call(gather_kernel, out_shape=jax.ShapeDtypeStruct((devices,) +...  31.2 us
    pallas_call x3, Pallas kernels, halo(): pl.pallas_call(functools.partial(halo_kernel, count), out_shape=jax.Shape...  22.4 us

commit v1 on v0

--- a/solution.py
+++ b/solution.py
@@ -158,58 +158,77 @@
 
 def gather_kernel(own, out, send_sem, recv_sem):
     axials, circs = lax.axis_size("axial"), lax.axis_size("circ")
-    devices = axials * circs
-    me = lax.axis_index("axial") * circs + lax.axis_index("circ")
-
-    def place(number):
-        return (number // circs, lax.rem(number, circs))
-
+    axial, circ = lax.axis_index("axial"), lax.axis_index("circ")
+    me = axial * circs + circ
+    greet(axial, circ, axials, circs)
+    exchange(own, out, send_sem, recv_sem)
+
+
+def greet(axial, circ, axials, circs):
     barrier = pltpu.get_barrier_semaphore()
-
-    def greet(step, carry):
+    for step in range(1, circs):
         pl.semaphore_signal(
-            barrier, inc=1, device_id=place(lax.rem(me + step, devices)), device_id_type=MESH
-        )
-        return carry
-
-    lax.fori_loop(1, devices, greet, 0)
-    pl.semaphore_wait(barrier, devices - 1)
-
-    def copy(step, slot):
+            barrier, inc=1, device_id=(axial, lax.rem(circ + step, circs)), device_id_type=MESH
+        )
+    for step in range(1, axials):
+        pl.semaphore_signal(
+            barrier, inc=1, device_id=(lax.rem(axial + step, axials), circ), device_id_type=MESH
+        )
+    pl.semaphore_wait(barrier, axials + circs - 2)
+
+
+def exchange(own, out, send_sem, recv_sem):
+    axials, circs = lax.axis_size("axial"), lax.axis_size("circ")
+    axial, circ = lax.axis_index("axial"), lax.axis_index("circ")
+    me = axial * circs + circ
+
+    def beside(step, slot):
         return pltpu.make_async_remote_copy(
             src_ref=own,
             dst_ref=out.at[slot],
             send_sem=send_sem.at[step],
             recv_sem=recv_sem.at[step],
-            device_id=place(lax.rem(me + step, devices)),
+            device_id=(axial, lax.rem(circ + step, circs)),
             device_id_type=MESH,
         )
 
-    def send(step, carry):
-        copy(step, me).start()
-        return carry
-
-    lax.fori_loop(1, devices, send, 0)
+    def along(step, cycle):
+        part = out.at[pl.ds(cycle * circs, circs)]
+        return pltpu.make_async_remote_copy(
+            src_ref=part,
+            dst_ref=part,
+            send_sem=send_sem.at[circs + step],
+            recv_sem=recv_sem.at[circs + step],
+            device_id=(lax.rem(axial + step, axials), circ),
+            device_id_type=MESH,
+        )
+
+    for step in range(1, circs):
+        beside(step, me).start()
     out[me] = own[...]
-
-    def finish(step, carry):
-        copy(step, lax.rem(me - step + devices, devices)).wait_recv()
-        copy(step, me).wait_send()
-        return carry
-
-    lax.fori_loop(1, devices, finish, 0)
+    for step in range(1, circs):
+        beside(step, axial * circs + lax.rem(circ - step + circs, circs)).wait_recv()
+    for step in range(1, axials):
+        along(step, axial).start()
+    for step in range(1, axials):
+        along(step, lax.rem(axial - step + axials, axials)).wait_recv()
+    for step in range(1, circs):
+        beside(step, me).wait_send()
+    for step in range(1, axials):
+        along(step, axial).wait_send()
 
 
 def gather(own, collective_id):
     devices = lax.axis_size("axial") * lax.axis_size("circ")
+    peers = lax.axis_size("axial") + lax.axis_size("circ")
     out = pl.pallas_call(
         gather_kernel,
         out_shape=jax.ShapeDtypeStruct((devices,) + own.shape, jnp.float32),
         in_specs=[VMEM],
         out_specs=VMEM,
         scratch_shapes=[
-            pltpu.SemaphoreType.DMA((devices,)),
-            pltpu.SemaphoreType.DMA((devices,)),
+            pltpu.SemaphoreType.DMA((peers,)),
+            pltpu.SemaphoreType.DMA((peers,)),
         ],
         compiler_params=params(collective_id),
         name="gather",
@@ -417,18 +436,77 @@
     panel[...] = result + in_sums([(len(PANELS) * LABELS, own)])
 
 
-def inverse_of(matrix):
-    size = matrix.shape[0]
-    line = lax.broadcasted_iota(jnp.int32, (size, size), 0)
-    column = lax.broadcasted_iota(jnp.int32, (size, size), 1)
-    for step in range(size):
-        pivot = 1.0 / matrix[step : step + 1, step : step + 1]
-        across = matrix[step : step + 1, :] * pivot
-        down = matrix[:, step : step + 1]
-        in_line, in_column = line == step, column == step
-        rest = jnp.where(in_column, 0.0, matrix) - down * jnp.where(in_column[0:1], pivot, across)
-        matrix = jnp.where(in_line, jnp.where(in_column, pivot, across), rest)
-    return matrix
+def inverse_two(a, b, c):
+    scale = 1.0 / (a * c - b * b)
+    return c * scale, -b * scale, a * scale
+
+
+def inverse_four(e):
+    a, b, c = inverse_two(e[0][0], e[1][0], e[1][1])
+    q = ((e[2][0], e[3][0]), (e[2][1], e[3][1]))
+    t = [[a * q[0][k] + b * q[1][k] for k in range(2)], [b * q[0][k] + c * q[1][k] for k in range(2)]]
+
+    def rest(i, k):
+        return e[2 + max(i, k)][2 + min(i, k)] - (q[0][i] * t[0][k] + q[1][i] * t[1][k])
+
+    x, y, z = inverse_two(rest(0, 0), rest(0, 1), rest(1, 1))
+    u = [[t[i][0] * x + t[i][1] * y, t[i][0] * y + t[i][1] * z] for i in range(2)]
+
+    def corner(i, k):
+        return u[i][0] * t[k][0] + u[i][1] * t[k][1]
+
+    across = b + corner(0, 1)
+    return [
+        [a + corner(0, 0), across, -u[0][0], -u[0][1]],
+        [across, c + corner(1, 1), -u[1][0], -u[1][1]],
+        [-u[0][0], -u[1][0], x, y],
+        [-u[0][1], -u[1][1], y, z],
+    ]
+
+
+def inverse_of(matrices):
+    size = matrices[0].shape[0]
+    tiles = size // 8
+    values = [matrix.reshape(tiles, 8, size) for matrix in matrices]
+    lane = lax.broadcasted_iota(jnp.int32, (1, 8, size), 2)
+    line = lax.broadcasted_iota(jnp.int32, (1, 8, size), 1)
+    wide = (tiles, 8, size)
+    for first in range(0, size, 4):
+        tile, sub = first // 8, first % 8
+        for number, value in enumerate(values):
+            columns = [
+                jnp.broadcast_to(value[:, :, first + k : first + k + 1], wide) for k in range(4)
+            ]
+            entries = [
+                [
+                    jnp.broadcast_to(columns[k][tile : tile + 1, sub + i : sub + i + 1, :], (1, 8, size))
+                    for k in range(i + 1)
+                ]
+                for i in range(4)
+            ]
+            rows = []
+            for i in range(4):
+                row = jnp.broadcast_to(value[tile : tile + 1, sub + i : sub + i + 1, :], (1, 8, size))
+                for k in range(4):
+                    row = jnp.where(lane == first + k, 1.0 if i == k else 0.0, row)
+                rows.append(row)
+            small = inverse_four(entries)
+            fresh = [
+                (small[i][0] * rows[0] + small[i][1] * rows[1])
+                + (small[i][2] * rows[2] + small[i][3] * rows[3])
+                for i in range(4)
+            ]
+            inside = jnp.logical_and(lane >= first, lane < first + 4)
+            left = jnp.where(inside, 0.0, value)
+            left = (left - columns[0] * fresh[0] - columns[1] * fresh[1]) - (
+                columns[2] * fresh[2] + columns[3] * fresh[3]
+            )
+            own = left[tile : tile + 1]
+            for i in range(4):
+                own = jnp.where(line == sub + i, fresh[i], own)
+            parts = [left[:tile]] * (tile > 0) + [own] + [left[tile + 1 :]] * (tile + 1 < tiles)
+            values[number] = jnp.concatenate(parts, axis=0)
+    return [value.reshape(size, size) for value in values]
 
 
 def coarse_kernel(cycles, gathered, inverse, diagonals, uppers, held, linked, partial):
@@ -462,7 +540,7 @@
         return jnp.where(unit_line + s * size == unit_column, 1.0, 0.0)
 
     def eliminate(s, s_next, upper):
-        inverted = inverse_of(diagonals[s])
+        inverted = inverse_of([diagonals[s]])[0]
         link = dot(inverted, upper)
         held[s] = inverted
         linked[s] = link
@@ -480,7 +558,7 @@
     def from_both_ends(step, carry):
         low, high = step, cycles - 1 - step
         upper_low, upper_high = uppers[low], uppers[high - 1].T
-        inverted_low, inverted_high = inverse_pair(diagonals[low], diagonals[high])
+        inverted_low, inverted_high = inverse_of([diagonals[low], diagonals[high]])
         for s, s_next, upper, inverted in (
             (low, low + 1, upper_low, inverted_low),
             (high, high - 1, upper_high, inverted_high),
@@ -495,7 +573,7 @@
     lax.fori_loop(0, middle - 1, from_both_ends, 0)
     eliminate(middle - 1, middle, uppers[middle - 1])
     rows = pl.ds(middle * size, size)
-    inverse[rows, :] = dot(inverse_of(diagonals[middle]), partial[middle])
+    inverse[rows, :] = dot(inverse_of([diagonals[middle]])[0], partial[middle])
 
     def put(s, s_next):
         ahead = inverse[pl.ds(s_next * size, size), :]
@@ -509,10 +587,6 @@
         return carry
 
     lax.fori_loop(0, middle - 1, back, 0)
-
-
-def inverse_pair(first, second):
-    return inverse_of(first), inverse_of(second)
 
 
 def coarse_inverse(gathered):

time: 130 us -> 110 us (0.85)
  Pallas kernels: 129 us -> 109 us
    pallas_call x1, Pallas kernels: 36.9 us -> 15.2 us  [coarse_inverse(): pl.pallas_call(functools.partial(coarse_kernel, cycles), out_shape=jax.Sh...]
    pallas_call x3, Pallas kernels: 31.2 us -> 34.2 us  [gather(): pl.pallas_call(gather_kernel, out_shape=jax.ShapeDtypeStruct((devices,) +...]
where the time goes in v1:
time: 110 us
  Pallas kernels  109 us (99%)
    pallas_call x6, Pallas kernels, call(): pl.pallas_call(kernel, out_shape=[jax.ShapeDtypeStruct(shape, jnp.float32...  38.3 us
    pallas_call x3, Pallas kernels, gather(): pl.pallas_call(gather_kernel, out_shape=jax.ShapeDtypeStruct((devices,) +...  34.2 us
    pallas_call x3, Pallas kernels, halo(): pl.pallas_call(functools.partial(halo_kernel, count), out_shape=jax.Shape...  21.6 us
    pallas_call x1, Pallas kernels, coarse_inverse(): pl.pallas_call(functools.partial(coarse_kernel, cycles), out_shape=jax.Sh...  15.2 us

profile of v1, /device:TPU:0, one launch (start us, length us, event | category | flops | bytes accessed | tf_op | source)
XLA Modules:
  0.0 109.9 jit_solution(14795061640729755365)
XLA Ops:
  0.6 8.8 %halo.3.ext.refs_1_.refs_2_ = f32[3,10,32,256]{3,2,1,0:T(8,128)} custom-call(f32[8,16,256]{2,1,0:T(8,128)} %refs_0_.1, s32[8,16,256]{2,1,0:T(8,128)} %refs_1_.1, s32[8,16,256]{2,1,0:T(8,128)} %refs_2_.1), custom_call_target="tpu_custom_call" | custom-call | tf_op jit(solution)/shard_map/halo/pallas_call | solution.py:144
  9.4 13.5 %weights.1 = (f32[27,8,16,256]{3,2,1,0:T(8,128)}, f32[8,128]{1,0:T(8,128)}) custom-call(f32[3,10,32,256]{3,2,1,0:T(8,128)} %halo.3.ext.refs_1_.refs_2_, f32[8,16,256]{2,1,0:T(8,128)} %right.3), custom_call_target="tpu_custom_call" | custom-call | tf_op jit(solution)/shard_map/weights/pallas_call | solution.py:732
  23.0 11.8 %gather.3 = f32[32,8,128]{2,1,0:T(8,128)} custom-call(f32[8,128]{1,0:T(8,128)} %get-tuple-element.15.own), custom_call_target="tpu_custom_call" | custom-call | tf_op jit(solution)/shard_map/gather/pallas_call | solution.py:224
  34.8 15.2 %coarse_inverse.1.inverse.refs_0_ = f32[256,256]{1,0:T(8,128)} custom-call(f32[256,128]{1,0:T(8,128)} %bitcast.3), custom_call_target="tpu_custom_call" | custom-call | tf_op jit(solution)/shard_map/coarse_inverse/pallas_call | solution.py:596
  50.0 5.0 %start.1 = (f32[8,16,256]{2,1,0:T(8,128)}, f32[8,16,256]{2,1,0:T(8,128)}) custom-call(f32[256,256]{1,0:T(8,128)} %coarse_inverse.1.inverse.refs_0_, f32[256,128]{1,0:T(8,128)} %bitcast.4, f32[3,10,32,256]{3,2,1,0:T(8,128)} %halo.3.ext.refs_1_.refs_2_, f32[27,8,16,256]{3,2,1,0:T(8,128)} %get-tuple-element.16.weights.refs_2_.refs_3_, f32[8,16,256]{2,1,0:T(8,128)} %right.3), custom_call_target="tpu_custom_call" | custom-call | tf_op jit(solution)/shard_map/start/pallas_call | solution.py:732
  54.9 6.4 %halo.4.refs_0_ = f32[1,10,32,256]{3,2,1,0:T(8,128)} custom-call(f32[8,16,256]{2,1,0:T(8,128)} %get-tuple-element.17.refs_0_.refs_5_), custom_call_target="tpu_custom_call" | custom-call | tf_op jit(solution)/shard_map/halo/pallas_call | solution.py:144
  61.3 4.5 %image.2 = (f32[8,16,256]{2,1,0:T(8,128)}, f32[8,128]{1,0:T(8,128)}) custom-call(f32[1,10,32,256]{3,2,1,0:T(8,128)} %halo.4.refs_0_, f32[3,10,32,256]{3,2,1,0:T(8,128)} %halo.3.ext.refs_1_.refs_2_, f32[27,8,16,256]{3,2,1,0:T(8,128)} %get-tuple-element.16.weights.refs_2_.refs_3_), custom_call_target="tpu_custom_call" | custom-call | tf_op jit(solution)/shard_map/image/pallas_call | solution.py:732
  65.8 11.5 %gather.4 = f32[32,8,128]{2,1,0:T(8,128)} custom-call(f32[8,128]{1,0:T(8,128)} %get-tuple-element.18.own), custom_call_target="tpu_custom_call" | custom-call | tf_op jit(solution)/shard_map/gather/pallas_call | solution.py:224
  77.3 5.4 %update.2 = (f32[8,16,256]{2,1,0:T(8,128)}, f32[8,16,256]{2,1,0:T(8,128)}, f32[8,16,256]{2,1,0:T(8,128)}, f32[8,16,256]{2,1,0:T(8,128)}, f32[8,128]{1,0:T(8,128)}) custom-call(f32[256,256]{1,0:T(8,128)} %coarse_inverse.1.inverse.refs_0_, f32[256,128]{1,0:T(8,128)} %bitcast.6, f32[3,10,32,256]{3,2,1,0:T(8,128)} %halo.3.ext.refs_1_.refs_2_, ...), custom_call_target="tpu_custom_call" | custom-call | tf_op jit(solution)/shard_map/update/pallas_call | solution.py:732
  82.7 6.4 %halo.5.refs_0_ = f32[1,10,32,256]{3,2,1,0:T(8,128)} custom-call(f32[8,16,256]{2,1,0:T(8,128)} %get-tuple-element.21.refs_0_.refs_5_), custom_call_target="tpu_custom_call" | custom-call | tf_op jit(solution)/shard_map/halo/pallas_call | solution.py:144
  89.2 4.5 %image.3 = (f32[8,16,256]{2,1,0:T(8,128)}, f32[8,128]{1,0:T(8,128)}) custom-call(f32[1,10,32,256]{3,2,1,0:T(8,128)} %halo.5.refs_0_, f32[3,10,32,256]{3,2,1,0:T(8,128)} %halo.3.ext.refs_1_.refs_2_, f32[27,8,16,256]{3,2,1,0:T(8,128)} %get-tuple-element.16.weights.refs_2_.refs_3_, f32[8,16,256]{2,1,0:T(8,128)} %get-tuple-element.22.refs_3_.refs_8_), custom_call_target="tpu_custom_call" | custom-call | tf_op jit(solution)/shard_map/image/pallas_call | solution.py:732
  93.7 10.9 %gather.5 = f32[32,8,128]{2,1,0:T(8,128)} custom-call(f32[8,128]{1,0:T(8,128)} %get-tuple-element.23.own), custom_call_target="tpu_custom_call" | custom-call | tf_op jit(solution)/shard_map/gather/pallas_call | solution.py:224
  104.5 5.4 %update.3 = (f32[8,16,256]{2,1,0:T(8,128)}, f32[8,16,256]{2,1,0:T(8,128)}) custom-call(f32[256,256]{1,0:T(8,128)} %coarse_inverse.1.inverse.refs_0_, f32[256,128]{1,0:T(8,128)} %bitcast.5, f32[3,10,32,256]{3,2,1,0:T(8,128)} %halo.3.ext.refs_1_.refs_2_, f32[27,8,16,256]{3,2,1,0:T(8,128)} %get-tuple-element.16.weights.refs_2_.refs_3_, ...), custom_call_target="tpu_custom_call" | custom-call | tf_op jit(solution)/shard_map/update/pallas_call | solution.py:732

commit v2 on v1

--- a/solution.py
+++ b/solution.py
@@ -45,71 +45,120 @@
     )
 
 
-def halo_kernel(count, *refs):
-    fields = refs[:count]
-    out, send_circ, send_axial, send_corner, recv_circ, recv_axial, recv_corner, send_sem, recv_sem = refs[count:]
+def wrapped(value, length):
+    return value - jnp.where(value >= length, length, 0)
+
+
+def for_others(action):
+    axials, circs = lax.axis_size("axial"), lax.axis_size("circ")
+    for c in range(1, circs):
+        action(0, c)
+
+    def row(a, carry):
+        for c in range(circs):
+            action(a, c)
+        return carry
+
+    lax.fori_loop(1, axials, row, 0)
+
+
+def other(a, c):
+    axials, circs = lax.axis_size("axial"), lax.axis_size("circ")
+    return (
+        wrapped(lax.axis_index("axial") + a, axials),
+        wrapped(lax.axis_index("circ") + c, circs),
+    )
+
+
+def greet():
+    barrier = pltpu.get_barrier_semaphore()
+
+    def signal(a, c):
+        pl.semaphore_signal(barrier, inc=1, device_id=other(a, c), device_id_type=MESH)
+
+    for_others(signal)
+
+
+def greeted():
+    devices = lax.axis_size("axial") * lax.axis_size("circ")
+    pl.semaphore_wait(pltpu.get_barrier_semaphore(), devices - 1)
+
+
+def inside(move):
+    at = lax.axis_index("axial") + move
+    return jnp.logical_and(at >= 0, at < lax.axis_size("axial"))
+
+
+def halo_buffers(count, block):
+    rows_axial, rows_circ, depth = block
+    buffers = [
+        pltpu.VMEM((2, count, rows_axial, depth), jnp.float32),
+        pltpu.VMEM((2, count, rows_circ, depth), jnp.float32),
+        pltpu.VMEM((4, count, 1, depth), jnp.float32),
+    ]
+    return buffers + buffers + [pltpu.SemaphoreType.DMA((len(SIDES),))] * 2
+
+
+def halo_copy(side, refs):
+    send_circ, send_axial, send_corner, recv_circ, recv_axial, recv_corner, send_sem, recv_sem = refs
+    circs = lax.axis_size("circ")
+    a, c = (side[0] + 1) // 2, (side[1] + 1) // 2
+    if side[0] == 0:
+        source, target = send_circ.at[c], recv_circ.at[1 - c]
+    elif side[1] == 0:
+        source, target = send_axial.at[a], recv_axial.at[1 - a]
+    else:
+        source, target = send_corner.at[2 * a + c], recv_corner.at[3 - 2 * a - c]
+    number = SIDES.index(side)
+    return pltpu.make_async_remote_copy(
+        src_ref=source,
+        dst_ref=target,
+        send_sem=send_sem.at[number],
+        recv_sem=recv_sem.at[number],
+        device_id=(
+            lax.axis_index("axial") + side[0],
+            wrapped(lax.axis_index("circ") + side[1] % circs, circs),
+        ),
+        device_id_type=MESH,
+    )
+
+
+def halo_send(fields, refs):
+    send_circ, send_axial, send_corner = refs[:3]
     rows_axial, rows_circ, depth = fields[0].shape
-    axials, circs = lax.axis_size("axial"), lax.axis_size("circ")
-    axial, circ = lax.axis_index("axial"), lax.axis_index("circ")
-
-    def inside(move):
-        return jnp.logical_and(axial + move >= 0, axial + move < axials)
-
-    def peer(side):
-        return (axial + side[0], lax.rem(circ + side[1] + circs, circs))
-
-    barrier = pltpu.get_barrier_semaphore()
+    for f, field in enumerate(fields):
+        for a in range(2):
+            x = a * (rows_axial - 1)
+            send_axial[a, f] = field[x].astype(jnp.float32)
+            for c in range(2):
+                row = c * (rows_circ - 1)
+                send_corner[2 * a + c, f] = field[x, row : row + 1, :].astype(jnp.float32)
+        for c in range(2):
+            row = c * (rows_circ - 1)
+            for x in range(rows_axial):
+                send_circ[c, f, x : x + 1, :] = field[x, row : row + 1, :].astype(jnp.float32)
+    greeted()
     for side in SIDES:
         @pl.when(inside(side[0]))
         def _():
-            pl.semaphore_signal(barrier, inc=1, device_id=peer(side), device_id_type=MESH)
-
-    for f in range(count):
-        value = fields[f][...].astype(jnp.float32)
-        send_axial[0, f] = value[0]
-        send_axial[1, f] = value[rows_axial - 1]
-        for c in range(2):
-            row = c * (rows_circ - 1)
-            face = value[:, row, :]
-            send_circ[c, f] = face
-            for a in range(2):
-                x = a * (rows_axial - 1)
-                send_corner[2 * a + c, f] = face[x : x + 1]
-
-    ends = jnp.where(axial == 0, 1, 0) + jnp.where(axial == axials - 1, 1, 0)
-    pl.semaphore_wait(barrier, len(SIDES) - 3 * ends)
-
-    def copy(side):
-        a, c = (side[0] + 1) // 2, (side[1] + 1) // 2
-        if side[0] == 0:
-            source, target = send_circ.at[c], recv_circ.at[1 - c]
-        elif side[1] == 0:
-            source, target = send_axial.at[a], recv_axial.at[1 - a]
-        else:
-            source, target = send_corner.at[2 * a + c], recv_corner.at[3 - 2 * a - c]
-        number = SIDES.index(side)
-        return pltpu.make_async_remote_copy(
-            src_ref=source,
-            dst_ref=target,
-            send_sem=send_sem.at[number],
-            recv_sem=recv_sem.at[number],
-            device_id=peer(side),
-            device_id_type=MESH,
-        )
-
-    for side in SIDES:
-        @pl.when(inside(side[0]))
-        def _():
-            copy(side).start()
-
-    for f in range(count):
+            halo_copy(side, refs).start()
+
+
+def halo_fill(fields, out):
+    rows_axial, rows_circ, depth = fields[0].shape
+    for f, field in enumerate(fields):
         for x in (0, rows_axial + 1):
             out[f, x] = jnp.zeros((rows_circ + 2 * PAD, depth), jnp.float32)
         blank = jnp.zeros((rows_axial, PAD, depth), jnp.float32)
         out[f, 1 : rows_axial + 1, 0:PAD, :] = blank
         out[f, 1 : rows_axial + 1, PAD + rows_circ :, :] = blank
-        out[f, 1 : rows_axial + 1, PAD : PAD + rows_circ, :] = fields[f][...].astype(jnp.float32)
-
+        out[f, 1 : rows_axial + 1, PAD : PAD + rows_circ, :] = field[...].astype(jnp.float32)
+
+
+def halo_receive(fields, out, refs):
+    recv_circ, recv_axial, recv_corner = refs[3:6]
+    rows_axial, rows_circ, depth = fields[0].shape
+    count = len(fields)
     edge = (PAD - 1, PAD + rows_circ)
     for side in SIDES:
         a, c = (1 - side[0]) // 2, (1 - side[1]) // 2
@@ -117,7 +166,7 @@
 
         @pl.when(inside(-side[0]))
         def _():
-            copy(side).wait_recv()
+            halo_copy(side, refs).wait_recv()
             for f in range(count):
                 if side[0] == 0:
                     for row in range(rows_axial):
@@ -130,110 +179,36 @@
     for side in SIDES:
         @pl.when(inside(side[0]))
         def _():
-            copy(side).wait_send()
-
-
-def halo(fields, collective_id):
-    count = len(fields)
-    rows_axial, rows_circ, depth = fields[0].shape
-    buffers = [
-        pltpu.VMEM((2, count, rows_axial, depth), jnp.float32),
-        pltpu.VMEM((2, count, rows_circ, depth), jnp.float32),
-        pltpu.VMEM((4, count, 1, depth), jnp.float32),
-    ]
-    return pl.pallas_call(
-        functools.partial(halo_kernel, count),
-        out_shape=jax.ShapeDtypeStruct(
-            (count, rows_axial + 2, rows_circ + 2 * PAD, depth), jnp.float32
-        ),
-        in_specs=[VMEM] * count,
-        out_specs=VMEM,
-        scratch_shapes=buffers
-        + buffers
-        + [pltpu.SemaphoreType.DMA((len(SIDES),)), pltpu.SemaphoreType.DMA((len(SIDES),))],
-        compiler_params=params(collective_id),
-        name="halo",
-    )(*fields)
-
-
-def gather_kernel(own, out, send_sem, recv_sem):
+            halo_copy(side, refs).wait_send()
+
+
+def gather(own, out, send_sem, recv_sem):
     axials, circs = lax.axis_size("axial"), lax.axis_size("circ")
-    axial, circ = lax.axis_index("axial"), lax.axis_index("circ")
-    me = axial * circs + circ
-    greet(axial, circ, axials, circs)
-    exchange(own, out, send_sem, recv_sem)
-
-
-def greet(axial, circ, axials, circs):
-    barrier = pltpu.get_barrier_semaphore()
-    for step in range(1, circs):
-        pl.semaphore_signal(
-            barrier, inc=1, device_id=(axial, lax.rem(circ + step, circs)), device_id_type=MESH
-        )
-    for step in range(1, axials):
-        pl.semaphore_signal(
-            barrier, inc=1, device_id=(lax.rem(axial + step, axials), circ), device_id_type=MESH
-        )
-    pl.semaphore_wait(barrier, axials + circs - 2)
-
-
-def exchange(own, out, send_sem, recv_sem):
-    axials, circs = lax.axis_size("axial"), lax.axis_size("circ")
-    axial, circ = lax.axis_index("axial"), lax.axis_index("circ")
-    me = axial * circs + circ
-
-    def beside(step, slot):
-        return pltpu.make_async_remote_copy(
+    me = lax.axis_index("axial") * circs + lax.axis_index("circ")
+
+    def send(a, c):
+        pltpu.make_async_remote_copy(
             src_ref=own,
-            dst_ref=out.at[slot],
-            send_sem=send_sem.at[step],
-            recv_sem=recv_sem.at[step],
-            device_id=(axial, lax.rem(circ + step, circs)),
+            dst_ref=out.at[me],
+            send_sem=send_sem,
+            recv_sem=recv_sem,
+            device_id=other(a, c),
             device_id_type=MESH,
-        )
-
-    def along(step, cycle):
-        part = out.at[pl.ds(cycle * circs, circs)]
-        return pltpu.make_async_remote_copy(
-            src_ref=part,
-            dst_ref=part,
-            send_sem=send_sem.at[circs + step],
-            recv_sem=recv_sem.at[circs + step],
-            device_id=(lax.rem(axial + step, axials), circ),
-            device_id_type=MESH,
-        )
-
-    for step in range(1, circs):
-        beside(step, me).start()
+        ).start()
+
+    for_others(send)
     out[me] = own[...]
-    for step in range(1, circs):
-        beside(step, axial * circs + lax.rem(circ - step + circs, circs)).wait_recv()
-    for step in range(1, axials):
-        along(step, axial).start()
-    for step in range(1, axials):
-        along(step, lax.rem(axial - step + axials, axials)).wait_recv()
-    for step in range(1, circs):
-        beside(step, me).wait_send()
-    for step in range(1, axials):
-        along(step, axial).wait_send()
-
-
-def gather(own, collective_id):
-    devices = lax.axis_size("axial") * lax.axis_size("circ")
-    peers = lax.axis_size("axial") + lax.axis_size("circ")
-    out = pl.pallas_call(
-        gather_kernel,
-        out_shape=jax.ShapeDtypeStruct((devices,) + own.shape, jnp.float32),
-        in_specs=[VMEM],
-        out_specs=VMEM,
-        scratch_shapes=[
-            pltpu.SemaphoreType.DMA((peers,)),
-            pltpu.SemaphoreType.DMA((peers,)),
-        ],
-        compiler_params=params(collective_id),
-        name="gather",
-    )(own)
-    return out.reshape(devices * LABELS, LANES)
+    most = out.at[pl.ds(0, axials * circs - 1)]
+    everything = pltpu.make_async_remote_copy(
+        src_ref=most,
+        dst_ref=most,
+        send_sem=send_sem,
+        recv_sem=recv_sem,
+        device_id=other(0, 1),
+        device_id_type=MESH,
+    )
+    everything.wait_recv()
+    everything.wait_send()
 
 
 def shifted(window, move):
@@ -284,8 +259,14 @@
     return jnp.sum(jnp.concatenate(rows, axis=0), axis=1, keepdims=True)
 
 
-def weights_kernel(ext, right, weights, panel, stiff, seen, total):
+def weights_kernel(stiffness, material_ref, groups_ref, right, ext, weights, gathered, panel, stiff, seen, total, gather_send, gather_recv, *halo_refs):
     rows_axial, rows_circ, depth = right.shape
+    greet()
+    fields = (stiffness, material_ref, groups_ref)
+    halo_send(fields, halo_refs)
+    halo_fill(fields, ext)
+    own = label_sums(ext.at[2], lambda x: right[x], rows_axial, rows_circ, depth)
+    halo_receive(fields, ext, halo_refs)
     groups = ext.at[2]
     half = len(HALF_STEPS)
 
@@ -432,8 +413,8 @@
         lines = jnp.dot(collect, jnp.where(same, total[slot], 0.0), precision=PRECISE)
         spots = jnp.where(spot_row // rows_circ + slot * LABELS == spot_column, 1.0, 0.0)
         result = result + jnp.dot(lines, spots, precision=PRECISE)
-    own = label_sums(groups, lambda x: right[x], rows_axial, rows_circ, depth)
     panel[...] = result + in_sums([(len(PANELS) * LABELS, own)])
+    gather(panel, gathered, gather_send, gather_recv)
 
 
 def inverse_two(a, b, c):
@@ -647,8 +628,10 @@
     lax.fori_loop(1, planes - 1, inner, 0)
 
 
-def start_kernel(inverse, gathered, ext, weights, right, solution, residual, values, spread):
+def start_kernel(inverse, gathered, ext, weights, right, solution, residual, image, sums_out, *refs):
+    values, spread, field, sums = refs[:4]
     rows_axial, rows_circ, depth = right.shape
+    greet()
     values[...] = jnp.dot(inverse[...], gathered[...], precision=PRECISE)
     spread_into(spread, values, len(PANELS) * LABELS, ext.at[2])
 
@@ -658,15 +641,16 @@
         return carry
 
     lax.fori_loop(0, rows_axial, plane, 0)
-
-
-def image_kernel(later, *refs):
-    if later:
-        residual_ext, ext, weights, direction_image, image, sums = refs
-    else:
-        residual_ext, ext, weights, image, sums = refs
+    image_sums(residual, field, ext, weights, None, image, sums, sums_out, refs[4:])
+
+
+def image_sums(residual_ref, field_ext, ext, weights, direction_image, image, sums, sums_out, refs):
+    later = direction_image is not None
+    halo_send((residual_ref,), refs[2:])
+    halo_fill((residual_ref,), field_ext)
+    halo_receive((residual_ref,), field_ext, refs[2:])
     rows_axial, rows_circ, depth = image.shape
-    field = residual_ext.at[0]
+    field = field_ext.at[0]
 
     def plane(x, totals):
         value = apply_plane(field, weights, x, rows_circ)
@@ -683,6 +667,7 @@
         whole = jnp.sum(jnp.sum(total, axis=0, keepdims=True), axis=1, keepdims=True)
         found.append((position + 1, jnp.where(line == 0, whole, 0.0)))
     sums[...] = in_sums(found)
+    gather(sums, sums_out, refs[0], refs[1])
 
 
 def update_kernel(later, final, *refs):
@@ -694,9 +679,10 @@
     solution_out, residual_out = refs[:2]
     refs = refs[2:]
     if not final:
-        direction_out, direction_image_out, scalars_out = refs[:3]
-        refs = refs[3:]
-    values, spread = refs
+        direction_out, direction_image_out, scalars_out, image_out, sums_out = refs[:5]
+        refs = refs[5:]
+        greet()
+    values, spread = refs[:2]
     rows_axial, rows_circ, depth = solution.shape
     values[...] = jnp.dot(inverse[...], gathered[...], precision=PRECISE)
     spread_into(spread, values, 0, ext.at[2])
@@ -726,16 +712,22 @@
     lax.fori_loop(0, rows_axial, plane, 0)
     if not final:
         scalars_out[...] = in_sums([(0, norm), (1, curvature)])
-
-
-def call(kernel, outs, scratch, args, name):
+        field, sums = refs[2:4]
+        image_sums(
+            residual_out, field, ext, weights, direction_image_out, image_out, sums, sums_out, refs[4:]
+        )
+
+
+def call(kernel, outs, scratch, args, name, collective_id=None):
     return pl.pallas_call(
         kernel,
         out_shape=[jax.ShapeDtypeStruct(shape, jnp.float32) for shape in outs],
         in_specs=[VMEM] * len(args),
         out_specs=[VMEM] * len(outs),
-        scratch_shapes=[pltpu.VMEM(shape, jnp.float32) for shape in scratch],
-        compiler_params=params(),
+        scratch_shapes=[
+            pltpu.VMEM(shape, jnp.float32) if isinstance(shape, tuple) else shape for shape in scratch
+        ],
+        compiler_params=params(collective_id),
         name=name,
     )(*args)
 
@@ -743,43 +735,51 @@
 def shards(right_side, stiffness, material, groups):
     block = right_side.shape
     rows_axial, rows_circ, depth = block
+    devices = lax.axis_size("axial") * lax.axis_size("circ")
     padded = (rows_axial + 2, rows_circ + 2 * PAD, depth)
     count = 2 * len(HALF_STEPS) + 1
     tile = (LABELS, LANES)
+    tiles = (devices,) + tile
+    flat = (devices * LABELS, LANES)
     size = LABELS * rows_circ
-    ext = halo([stiffness, material, groups], 0)
-    weights, panel = call(
+    pair = [pltpu.SemaphoreType.DMA, pltpu.SemaphoreType.DMA]
+    ext, weights, gathered = call(
         weights_kernel,
-        [(count,) + block, tile],
-        [(len(HALF_STEPS),) + padded, (count, rows_circ, depth), (len(PANELS), size, size)],
-        [ext, right_side],
+        [(3,) + padded, (count,) + block, tiles],
+        [tile, (len(HALF_STEPS),) + padded, (count, rows_circ, depth), (len(PANELS), size, size)]
+        + pair
+        + halo_buffers(3, block),
+        [stiffness, material, groups, right_side],
         "weights",
+        0,
     )
-    gathered = gather(panel, 1)
+    gathered = gathered.reshape(flat)
     inverse = coarse_inverse(gathered)
-    work = [gathered.shape, padded]
-    solution, residual = call(
-        start_kernel, [block, block], work, [inverse, gathered, ext, weights, right_side], "start"
+    work = [flat, padded]
+    talk = [(1,) + padded, tile] + pair + halo_buffers(1, block)
+    solution, residual, image, sums = call(
+        start_kernel,
+        [block, block, block, tiles],
+        work + talk,
+        [inverse, gathered, ext, weights, right_side],
+        "start",
+        1,
     )
     carried = []
     for iteration in range(ITERS):
         later, final = iteration > 0, iteration + 1 == ITERS
-        residual_ext = halo([residual], 2 + 2 * iteration)
-        image, sums = call(
-            functools.partial(image_kernel, later),
-            [block, tile],
-            [],
-            [residual_ext, ext, weights] + carried[1:2],
-            "image",
-        )
-        gathered = gather(sums, 3 + 2 * iteration)
+        outs = [block, block] + ([] if final else [block, block, tile, block, tiles])
         solution, residual, *carried = call(
             functools.partial(update_kernel, later, final),
-            [block, block] + ([] if final else [block, block, tile]),
-            work,
-            [inverse, gathered, ext, weights, solution, residual, image] + carried,
+            outs,
+            work + ([] if final else talk),
+            [inverse, sums.reshape(flat), ext, weights, solution, residual, image] + carried,
             "update",
+            None if final else 2 + iteration,
         )
+        if not final:
+            image, sums = carried[3:]
+            carried = carried[:3]
     return (solution, residual)
 
 

time: 110 us -> 83.2 us (0.76)
  Pallas kernels: 109 us -> 82.4 us
    pallas_call x6 -> x0, Pallas kernels: 55.8 us -> none  [the longest x3 34.2 us: gather(): pl.pallas_call(gather_kernel, out_shape=jax.ShapeDtypeStruct((devices,) +...]
    pallas_call x6 -> x4, Pallas kernels: 38.3 us -> 67.3 us  [call(): pl.pallas_call(kernel, out_shape=[jax.ShapeDtypeStruct(shape, jnp.float32...]
where the time goes in v2:
time: 83.2 us; the launch traced here: 83.1 us
  Pallas kernels  82.4 us (99%)
    pallas_call x4, Pallas kernels, call(): pl.pallas_call(kernel, out_shape=[jax.ShapeDtypeStruct(shape, jnp.float32...  67.3 us
    pallas_call x1, Pallas kernels, coarse_inverse(): pl.pallas_call(functools.partial(coarse_kernel, cycles), out_shape=jax.Sh...  15.2 us

profile of v2, /device:TPU:0, one launch (start us, length us, event | category | flops | bytes accessed | tf_op | source)
XLA Modules:
  0.0 83.1 jit_solution(14133399424973198254)
XLA Ops:
  0.6 28.1 %weights.1 = (f32[3,10,32,256]{3,2,1,0:T(8,128)}, f32[27,8,16,256]{3,2,1,0:T(8,128)}, f32[32,8,128]{2,1,0:T(8,128)}) custom-call(f32[8,16,256]{2,1,0:T(8,128)} %stiffness.1, s32[8,16,256]{2,1,0:T(8,128)} %material_ref.1, s32[8,16,256]{2,1,0:T(8,128)} %groups_ref.1, f32[8,16,256]{2,1,0:T(8,128)} %right.3), custom_call_target="tpu_custom_call" | custom-call | tf_op jit(solution)/shard_map/weights/pallas_call | solution.py:722
  28.7 15.2 %coarse_inverse.1.inverse.refs_0_ = f32[256,256]{1,0:T(8,128)} custom-call(f32[256,128]{1,0:T(8,128)} %bitcast.3), custom_call_target="tpu_custom_call" | custom-call | tf_op jit(solution)/shard_map/coarse_inverse/pallas_call | solution.py:577
  43.9 16.9 %start.1 = (f32[8,16,256]{2,1,0:T(8,128)}, f32[8,16,256]{2,1,0:T(8,128)}, f32[8,16,256]{2,1,0:T(8,128)}, f32[32,8,128]{2,1,0:T(8,128)}) custom-call(f32[256,256]{1,0:T(8,128)} %coarse_inverse.1.inverse.refs_0_, f32[256,128]{1,0:T(8,128)} %bitcast.4, f32[3,10,32,256]{3,2,1,0:T(8,128)} %get-tuple-element.17.ext.refs_2_, ...), custom_call_target="tpu_custom_call" | custom-call | tf_op jit(solution)/shard_map/start/pallas_call | solution.py:722
  60.8 16.9 %update.2 = (f32[8,16,256]{2,1,0:T(8,128)}, f32[8,16,256]{2,1,0:T(8,128)}, f32[8,16,256]{2,1,0:T(8,128)}, f32[8,16,256]{2,1,0:T(8,128)}, f32[8,128]{1,0:T(8,128)...) custom-call(f32[256,256]{1,0:T(8,128)} %coarse_inverse.1.inverse.refs_0_, f32[256,128]{1,0:T(8,128)} %bitcast.6, ...), custom_call_target="tpu_custom_call" | custom-call | tf_op jit(solution)/shard_map/update/pallas_call | solution.py:722
  77.7 5.4 %update.3 = (f32[8,16,256]{2,1,0:T(8,128)}, f32[8,16,256]{2,1,0:T(8,128)}) custom-call(f32[256,256]{1,0:T(8,128)} %coarse_inverse.1.inverse.refs_0_, f32[256,128]{1,0:T(8,128)} %bitcast.5, f32[3,10,32,256]{3,2,1,0:T(8,128)} %get-tuple-element.17.ext.refs_2_, f32[27,8,16,256]{3,2,1,0:T(8,128)} %get-tuple-element.18.weights.refs_3_, ...), custom_call_target="tpu_custom_call" | custom-call | tf_op jit(solution)/shard_map/update/pallas_call | solution.py:722

commit v3 on v2

--- a/solution.py
+++ b/solution.py
@@ -259,7 +259,7 @@
     return jnp.sum(jnp.concatenate(rows, axis=0), axis=1, keepdims=True)
 
 
-def weights_kernel(stiffness, material_ref, groups_ref, right, ext, weights, gathered, panel, stiff, seen, total, gather_send, gather_recv, *halo_refs):
+def weights_kernel(stiffness, material_ref, groups_ref, right, ext, weights, gathered, panel, stiff, seen, gather_send, gather_recv, *halo_refs):
     rows_axial, rows_circ, depth = right.shape
     greet()
     fields = (stiffness, material_ref, groups_ref)
@@ -315,104 +315,106 @@
     lax.fori_loop(0, rows_axial, weight_plane, 0)
 
     row = lax.broadcasted_iota(jnp.int32, (rows_circ, depth), 0)
-    listed = terms()
-    total[...] = jnp.zeros_like(total)
-
-    def own_labels(x):
-        labels = window_of(groups, x, rows_circ, (0, 0))
+    last = rows_axial - 1
+
+    def one_hot(labels):
         return jnp.concatenate(
             [jnp.where(labels == float(label), 1.0, 0.0) for label in range(LABELS)], axis=0
         )
 
-    def seen_labels(offset, x):
-        labels = window_of(groups, x, rows_circ, offset)
-        if offset[2] == 0:
+    def moved(labels, move):
+        if move == 0:
             return labels
         lane = lax.broadcasted_iota(jnp.int32, labels.shape, 1)
-        rolled = pltpu.roll(labels, (depth - offset[2]) % depth, 1)
-        return jnp.where(lane == (depth - 1 if offset[2] > 0 else 0), -1.0, rolled)
-
-    def add_panel(slot, x, parts):
-        found = jnp.concatenate(parts, axis=0)
-        total[slot] += lax.dot_general(
-            own_labels(x),
-            found,
+        rolled = pltpu.roll(labels, (depth - move) % depth, 1)
+        return jnp.where(lane == (depth - 1 if move > 0 else 0), -1.0, rolled)
+
+    def seen_labels(offset, x):
+        return moved(window_of(groups, x, rows_circ, offset), offset[2])
+
+    def pair_sums(labels, parts):
+        return lax.dot_general(
+            one_hot(labels),
+            jnp.concatenate(parts, axis=0),
             (((1,), (1,)), ((), ())),
             precision=PRECISE,
             preferred_element_type=jnp.float32,
         )
 
-    def panel_plane(x, carry):
-        for number, (position, offset) in enumerate(listed):
+    def panel_plane(x, total):
+        for position, offset in enumerate(HALF_STEPS):
             labels = seen_labels(offset, x)
-            leaves = None
+            if offset[0] != 0:
+                labels = jnp.where(x == last, -1.0, labels)
             if offset[1] != 0:
                 leaves = row == (rows_circ - 1 if offset[1] > 0 else 0)
-            if offset[0] != 0:
-                edge = x == (rows_axial - 1 if offset[0] > 0 else 0)
-                labels = jnp.where(edge, -1.0, labels)
-            seen[number] = labels if leaves is None else jnp.where(leaves, -1.0, labels)
-        parts, beside = [], []
-        centre = window_of(groups, x, rows_circ, (0, 0))
-        for label in range(LABELS):
-            found = jnp.where(centre == float(label), weights[2 * half, x], 0.0)
-            for number, (position, offset) in enumerate(listed):
-                found = found - jnp.where(seen[number] == float(label), weights[position, x], 0.0)
-            parts.append(found)
-        add_panel(0, x, parts)
-        for number, (position, offset) in enumerate(listed):
-            if offset[1] > 0:
-                labels = seen_labels(offset, x)
-                if offset[0] != 0:
-                    edge = x == (rows_axial - 1 if offset[0] > 0 else 0)
-                    labels = jnp.where(edge, -1.0, labels)
-                seen[number] = jnp.where(row == rows_circ - 1, labels, -1.0)
+                labels = jnp.where(leaves, -1.0, labels)
+            seen[position] = labels
+        parts = []
         for label in range(LABELS):
             found = jnp.zeros((rows_circ, depth), jnp.float32)
-            for number, (position, offset) in enumerate(listed):
-                if offset[1] > 0:
-                    found = found - jnp.where(
-                        seen[number] == float(label), weights[position, x], 0.0
-                    )
-            beside.append(found)
-        add_panel(1, x, beside)
-        return carry
-
-    lax.fori_loop(0, rows_axial, panel_plane, 0)
-
-    last = rows_axial - 1
+            for position in range(half):
+                found = found - jnp.where(seen[position] == float(label), weights[position, x], 0.0)
+            parts.append(found)
+        return total + pair_sums(window_of(groups, x, rows_circ, (0, 0)), parts)
+
+    size = LABELS * rows_circ
+    totals = [lax.fori_loop(0, rows_axial, panel_plane, jnp.zeros((size, size), jnp.float32))]
+
+    plane = lax.broadcasted_iota(jnp.int32, (rows_axial, depth), 0)
+    chosen = []
+    for position, offset in terms():
+        if offset[1] > 0:
+            first = 1 + offset[0]
+            labels = moved(groups[first : first + rows_axial, PAD + rows_circ, :], offset[2])
+            if offset[0] != 0:
+                labels = jnp.where(plane == (last if offset[0] > 0 else 0), -1.0, labels)
+            chosen.append((labels, weights[position, :, rows_circ - 1, :]))
+
+    def panel_of(chosen, shape):
+        parts = []
+        for label in range(LABELS):
+            found = jnp.zeros(shape, jnp.float32)
+            for labels, weight in chosen:
+                found = found - jnp.where(labels == float(label), weight, 0.0)
+            parts.append(found)
+        return parts
+
+    beside = groups[1 : 1 + rows_axial, PAD + rows_circ - 1, :]
+    totals.append(pair_sums(beside, panel_of(chosen, (rows_axial, depth))))
+
     for slot in range(2, len(PANELS)):
         move = PANELS[slot][1]
         chosen = []
-        for position, offset in listed:
+        for position, offset in enumerate(HALF_STEPS):
             if offset[0] > 0 and (offset[1] == move or move == 0):
                 labels = seen_labels(offset, last)
                 if offset[1] != 0:
                     leaves = row == (rows_circ - 1 if offset[1] > 0 else 0)
                     labels = jnp.where(leaves == (move != 0), labels, -1.0)
-                chosen.append((position, labels))
-        parts = []
-        for label in range(LABELS):
-            found = jnp.zeros((rows_circ, depth), jnp.float32)
-            for position, labels in chosen:
-                found = found - jnp.where(labels == float(label), weights[position, last], 0.0)
-            parts.append(found)
-        add_panel(slot, last, parts)
-
-    size = LABELS * rows_circ
-    line = lax.broadcasted_iota(jnp.int32, (size, size), 0)
-    column = lax.broadcasted_iota(jnp.int32, (size, size), 1)
-    same = lax.rem(line, rows_circ) == lax.rem(column, rows_circ)
-    tile_row = lax.broadcasted_iota(jnp.int32, (LABELS, size), 0)
-    tile_column = lax.broadcasted_iota(jnp.int32, (LABELS, size), 1)
-    collect = jnp.where(tile_column // rows_circ == tile_row, 1.0, 0.0)
-    spot_row = lax.broadcasted_iota(jnp.int32, (size, LANES), 0)
-    spot_column = lax.broadcasted_iota(jnp.int32, (size, LANES), 1)
+                chosen.append((labels, weights[position, last]))
+        centre = window_of(groups, last, rows_circ, (0, 0))
+        totals.append(pair_sums(centre, panel_of(chosen, (rows_circ, depth))))
+
     result = jnp.zeros((LABELS, LANES), jnp.float32)
-    for slot in range(len(PANELS)):
-        lines = jnp.dot(collect, jnp.where(same, total[slot], 0.0), precision=PRECISE)
-        spots = jnp.where(spot_row // rows_circ + slot * LABELS == spot_column, 1.0, 0.0)
+    for slot, total in enumerate(totals):
+        size = total.shape[0]
+        rows = size // LABELS
+        line = lax.broadcasted_iota(jnp.int32, (size, size), 0)
+        column = lax.broadcasted_iota(jnp.int32, (size, size), 1)
+        same = lax.rem(line, rows) == lax.rem(column, rows)
+        tile_row = lax.broadcasted_iota(jnp.int32, (LABELS, size), 0)
+        tile_column = lax.broadcasted_iota(jnp.int32, (LABELS, size), 1)
+        collect = jnp.where(tile_column // rows == tile_row, 1.0, 0.0)
+        spot_row = lax.broadcasted_iota(jnp.int32, (size, LANES), 0)
+        spot_column = lax.broadcasted_iota(jnp.int32, (size, LANES), 1)
+        spots = jnp.where(spot_row // rows + slot * LABELS == spot_column, 1.0, 0.0)
+        lines = jnp.dot(collect, jnp.where(same, total, 0.0), precision=PRECISE)
         result = result + jnp.dot(lines, spots, precision=PRECISE)
+    centre = label_sums(groups, lambda x: weights[2 * half, x], rows_axial, rows_circ, depth)
+    spot_row = lax.broadcasted_iota(jnp.int32, (LABELS, LANES), 0)
+    spot_column = lax.broadcasted_iota(jnp.int32, (LABELS, LANES), 1)
+    result = result + jnp.where(spot_row == spot_column, 0.5 * centre, 0.0)
     panel[...] = result + in_sums([(len(PANELS) * LABELS, own)])
     gather(panel, gathered, gather_send, gather_recv)
 
@@ -494,26 +496,25 @@
     size = gathered.shape[0] // cycles
     whole = gathered.shape[0]
     circs = size // LABELS
-    line = lax.broadcasted_iota(jnp.int32, (size, size), 0) // LABELS
-    column = lax.broadcasted_iota(jnp.int32, (size, size), 1) // LABELS
     spread_row = lax.broadcasted_iota(jnp.int32, (LANES, size), 0)
     spread_column = lax.rem(lax.broadcasted_iota(jnp.int32, (LANES, size), 1), LABELS)
+    line = lax.rem(lax.broadcasted_iota(jnp.int32, (whole, size), 0) // LABELS, circs)
+    column = lax.broadcasted_iota(jnp.int32, (whole, size), 1) // LABELS
 
     def dot(left, right):
         return jnp.dot(left, right, precision=PRECISE, preferred_element_type=jnp.float32)
 
-    def block(s, slot):
+    def blocks(slot):
         tiles = jnp.where(spread_row == spread_column + slot * LABELS, 1.0, 0.0)
-        placed = dot(gathered[pl.ds(s * size, size), :], tiles)
+        placed = dot(gathered[...], tiles)
         return jnp.where(lax.rem(line + PANELS[slot][1] + circs, circs) == column, placed, 0.0)
 
-    def assemble(s, carry):
-        beside = block(s, 1)
-        diagonals[s] = block(s, 0) + beside + beside.T
-        uppers[s] = block(s, 2) + block(s, 3) + block(s, 4)
-        return carry
-
-    lax.fori_loop(0, cycles, assemble, 0)
+    own = blocks(0) + blocks(1)
+    ahead = blocks(2) + blocks(3) + blocks(4)
+    for s in range(cycles):
+        part = own[s * size : (s + 1) * size]
+        diagonals[s] = part + part.T
+        uppers[s] = ahead[s * size : (s + 1) * size]
     unit_line = lax.broadcasted_iota(jnp.int32, (size, whole), 0)
     unit_column = lax.broadcasted_iota(jnp.int32, (size, whole), 1)
 
@@ -551,7 +552,7 @@
             partial[s_next] = partial[s_next] - dot(link.T, partial[s])
         return carry
 
-    lax.fori_loop(0, middle - 1, from_both_ends, 0)
+    lax.fori_loop(0, middle - 1, from_both_ends, 0, unroll=whole <= 256)
     eliminate(middle - 1, middle, uppers[middle - 1])
     rows = pl.ds(middle * size, size)
     inverse[rows, :] = dot(inverse_of([diagonals[middle]])[0], partial[middle])
@@ -567,7 +568,7 @@
         put(middle + 1 + step, middle + step)
         return carry
 
-    lax.fori_loop(0, middle - 1, back, 0)
+    lax.fori_loop(0, middle - 1, back, 0, unroll=whole <= 256)
 
 
 def coarse_inverse(gathered):
@@ -741,12 +742,11 @@
     tile = (LABELS, LANES)
     tiles = (devices,) + tile
     flat = (devices * LABELS, LANES)
-    size = LABELS * rows_circ
     pair = [pltpu.SemaphoreType.DMA, pltpu.SemaphoreType.DMA]
     ext, weights, gathered = call(
         weights_kernel,
         [(3,) + padded, (count,) + block, tiles],
-        [tile, (len(HALF_STEPS),) + padded, (count, rows_circ, depth), (len(PANELS), size, size)]
+        [tile, (len(HALF_STEPS),) + padded, (len(HALF_STEPS), rows_circ, depth)]
         + pair
         + halo_buffers(3, block),
         [stiffness, material, groups, right_side],

time: 83.2 us -> 78.6 us (0.945)
  Pallas kernels: 82.4 us -> 77.8 us
    pallas_call x1, Pallas kernels: 15.2 us -> 12.8 us  [coarse_inverse(): pl.pallas_call(functools.partial(coarse_kernel, cycles), out_shape=jax.Sh...]
    pallas_call x4, Pallas kernels: 67.3 us -> 65 us  [call(): pl.pallas_call(kernel, out_shape=[jax.ShapeDtypeStruct(shape, jnp.float32...]
where the time goes in v3:
time: 78.6 us; the launch traced here: 78.5 us
  Pallas kernels  77.8 us (99%)
    pallas_call x4, Pallas kernels, call(): pl.pallas_call(kernel, out_shape=[jax.ShapeDtypeStruct(shape, jnp.float32...  65 us
    pallas_call x1, Pallas kernels, coarse_inverse(): pl.pallas_call(functools.partial(coarse_kernel, cycles), out_shape=jax.Sh...  12.8 us

profile of v3, /device:TPU:0, one launch (start us, length us, event | category | flops | bytes accessed | tf_op | source)
XLA Modules:
  0.0 78.5 jit_solution(14188383896502226885)
XLA Ops:
  0.6 25.9 %weights.1 = (f32[3,10,32,256]{3,2,1,0:T(8,128)}, f32[27,8,16,256]{3,2,1,0:T(8,128)}, f32[32,8,128]{2,1,0:T(8,128)}) custom-call(f32[8,16,256]{2,1,0:T(8,128)} %stiffness.1, s32[8,16,256]{2,1,0:T(8,128)} %material_ref.1, s32[8,16,256]{2,1,0:T(8,128)} %groups_ref.1, f32[8,16,256]{2,1,0:T(8,128)} %right.3), custom_call_target="tpu_custom_call" | custom-call | tf_op jit(solution)/shard_map/weights/pallas_call | solution.py:723
  26.5 12.8 %coarse_inverse.1.inverse.refs_0_ = f32[256,256]{1,0:T(8,128)} custom-call(f32[256,128]{1,0:T(8,128)} %bitcast.3), custom_call_target="tpu_custom_call" | custom-call | tf_op jit(solution)/shard_map/coarse_inverse/pallas_call | solution.py:578
  39.3 16.9 %start.1 = (f32[8,16,256]{2,1,0:T(8,128)}, f32[8,16,256]{2,1,0:T(8,128)}, f32[8,16,256]{2,1,0:T(8,128)}, f32[32,8,128]{2,1,0:T(8,128)}) custom-call(f32[256,256]{1,0:T(8,128)} %coarse_inverse.1.inverse.refs_0_, f32[256,128]{1,0:T(8,128)} %bitcast.4, f32[3,10,32,256]{3,2,1,0:T(8,128)} %get-tuple-element.17.ext.refs_2_, ...), custom_call_target="tpu_custom_call" | custom-call | tf_op jit(solution)/shard_map/start/pallas_call | solution.py:723
  56.2 16.9 %update.2 = (f32[8,16,256]{2,1,0:T(8,128)}, f32[8,16,256]{2,1,0:T(8,128)}, f32[8,16,256]{2,1,0:T(8,128)}, f32[8,16,256]{2,1,0:T(8,128)}, f32[8,128]{1,0:T(8,128)...) custom-call(f32[256,256]{1,0:T(8,128)} %coarse_inverse.1.inverse.refs_0_, f32[256,128]{1,0:T(8,128)} %bitcast.6, ...), custom_call_target="tpu_custom_call" | custom-call | tf_op jit(solution)/shard_map/update/pallas_call | solution.py:723
  73.1 5.4 %update.3 = (f32[8,16,256]{2,1,0:T(8,128)}, f32[8,16,256]{2,1,0:T(8,128)}) custom-call(f32[256,256]{1,0:T(8,128)} %coarse_inverse.1.inverse.refs_0_, f32[256,128]{1,0:T(8,128)} %bitcast.5, f32[3,10,32,256]{3,2,1,0:T(8,128)} %get-tuple-element.17.ext.refs_2_, f32[27,8,16,256]{3,2,1,0:T(8,128)} %get-tuple-element.18.weights.refs_3_, ...), custom_call_target="tpu_custom_call" | custom-call | tf_op jit(solution)/shard_map/update/pallas_call | solution.py:723
